TPU v7x, 32 devices: a whole 2x2x4 slice. The times are simulated.
32 devices in a mesh: leaf: 8 (over z, x), row: 4 (over y, core).
Axes of the slice: x: 2, y: 2, z: 4, core: 2. Of those that a mesh axis runs over, the one named last changes fastest.
Arguments:
- sec_rhs: float32 [64, 4096], P(None, ('leaf', 'row')), may hold values from -6 to 6
- sec_inverse: float32 [4096, 512], P(('leaf', 'row')), as said below
- sep_rhs: float32 [4, 64, 1024], P(None, None, 'leaf'), may hold values from -6 to 6
- sep_inverse: float32 [4, 1024, 1024], P(None, 'leaf'), as said below
- sep_coupling: float32 [3, 1024, 1024], P(None, 'leaf'), may hold values from -0.1875 to 0.1875
- sec_update: float32 [4, 1024, 4096], P(None, None, ('leaf', 'row')), may hold values from -0.1875 to 0.1875
- link: int32 [8, 4], P('leaf'), may hold values 0 or 1
Outputs:
- sec_solution: float32 [64, 4096], P(None, ('leaf', 'row'))
- sep_solution: float32 [4, 64, 1024], P(None, None, 'leaf')
Inputs may be any that keep to these rules, and one draw needn't show every extreme that they name: link holds only 0 and 1. Each section's block of sec_inverse is lower triangular with entries on the diagonal between 0.7 and 1.3. Each block of sep_inverse is lower triangular with entries on the diagonal between 0.7 and 1.3.
All inputs are finite; a program needn't handle non-finite values. No bound on the sum of `link` on one device may be relied on, other than what follows from the above.
Results may differ from a plain program's by a relative error of at most 0.00013.
Values sent between devices are 32-bit elements; how exact they have to be, the bound alone decides.
A program may use at most 128 MiB of HBM per device.

v0:
```python
import jax
import jax.numpy as jnp
from jax import lax
from jax.sharding import PartitionSpec as P


def dot_last(left, right):
    return lax.dot_general(
        left,
        right,
        (((1,), (1,)), ((), ())),
        precision=lax.Precision.HIGHEST,
        preferred_element_type=jnp.float32,
    )


def dot_plain(left, right):
    return jnp.dot(left, right, precision=lax.Precision.HIGHEST, preferred_element_type=jnp.float32)


def per_device(sec_rhs, sec_inverse, sep_rhs, sep_inverse, sep_coupling, sec_update, link):
    highest = lax.Precision.HIGHEST
    levels = sep_rhs.shape[0]
    link_weights = link[0].astype(jnp.float32)
    rhs_full = lax.all_gather(sec_rhs, "row", axis=1, tiled=True)
    y_sec = dot_last(rhs_full, sec_inverse)
    section_parts = (
        jnp.einsum("rj,kmj->krm", y_sec, sec_update, precision=highest)
        * link_weights[:, None, None]
    )
    row_total = lax.psum(section_parts, "row")
    reduced = lax.psum_scatter(row_total, "leaf", scatter_dimension=2, tiled=True)
    y_leaf = []
    y_full = None
    for level in range(levels):
        known_part = sep_rhs[level] - reduced[level]
        if level > 0:
            known_part = known_part - dot_last(y_full, sep_coupling[level - 1])
        known_full = lax.all_gather(known_part, "leaf", axis=1, tiled=True)
        y_level = dot_last(known_full, sep_inverse[level])
        y_leaf.append(y_level)
        if level < levels - 1:
            y_full = lax.all_gather(y_level, "leaf", axis=1, tiled=True)
    solved = [None] * levels
    rhs_width = y_leaf[0].shape[0] // lax.axis_size("row")
    rhs_start = lax.axis_index("row") * rhs_width
    for level in range(levels - 1, -1, -1):
        adjusted = lax.dynamic_slice_in_dim(y_leaf[level], rhs_start, rhs_width, 0)
        if level < levels - 1:
            coupling_part = dot_plain(solved[level + 1], sep_coupling[level])
            adjusted = adjusted - lax.psum_scatter(
                coupling_part, "leaf", scatter_dimension=1, tiled=True
            )
        solve_part = dot_plain(adjusted, sep_inverse[level])
        solved[level] = lax.psum_scatter(solve_part, "leaf", scatter_dimension=1, tiled=True)
    solved_stack = lax.all_gather(jnp.stack(solved), "row", axis=1, tiled=True)
    solved_full = lax.all_gather(solved_stack, "leaf", axis=2, tiled=True)
    weighted = solved_full * link_weights[:, None, None]
    back_sec = y_sec - jnp.einsum("krm,kmj->rj", weighted, sec_update, precision=highest)
    section_part = dot_plain(back_sec, sec_inverse)
    sec_solution = lax.psum_scatter(section_part, "row", scatter_dimension=1, tiled=True)
    return (sec_solution, solved_stack)


def solution(mesh):
    in_specs = (
        P(None, ("leaf", "row")),
        P(("leaf", "row"), None),
        P(None, None, "leaf"),
        P(None, "leaf", None),
        P(None, "leaf", None),
        P(None, None, ("leaf", "row")),
        P("leaf", None),
    )
    out_specs = (P(None, ("leaf", "row")), P(None, None, "leaf"))
    return jax.shard_map(
        per_device, mesh=mesh, in_specs=in_specs, out_specs=out_specs, check_vma=False
    )
```

profile of v0, /device:TPU:0, one launch (start us, length us, event | category | flops | bytes accessed | tf_op | source)
XLA Modules:
  0.0 811.1 jit_solution(3679977903072324729)
XLA Ops:
  7.2 0.0 reduce-scatter.26.cloned.1.call-start
  7.2 6.9 all_gather.30
  14.1 0.7 convert_bitcast_fusion
  14.7 1.3 fusion.59
  16.1 3.3 fusion
  19.5 0.0 reduce-scatter.26.cloned.1.call-update
  19.5 0.0 all-reduce.2.cloned.1.call-start
  19.5 65.5 %reduce-scatter.26.cloned.1.call-done = f32[4,64,128]{2,1,0:T(8,128)} async-done(((f32[4,64,1024]{2,1,0:T(8,128)}), f32[4,64,128]{2,1,0:T(8,128)}) %reduce-scatter.26.cloned.1.call-update) | async-done | bytes 131088 | tf_op jit(solution)/shard_map/reduce_scatter | solution.py:32
  85.1 0.0 all-reduce.2.cloned.1.call-update
  85.1 0.0 reduce-scatter.10.cloned.1.call-start
  85.1 32.8 %all-reduce.2.cloned.1.call-done = f32[4,64,128]{2,1,0:T(8,128)} async-done(((f32[4,64,128]{2,1,0:T(8,128)}), f32[4,64,128]{2,1,0:T(8,128)}) %all-reduce.2.cloned.1.call-update) | async-done | bytes 131088 | tf_op jit(solution)/shard_map/psum | solution.py:31
  118.0 0.9 slice_subtract_fusion.3
  118.9 31.0 %all-gather = f32[1,64,1024]{2,1,0:T(8,128)S(1)} all-gather(f32[1,64,128]{2,1,0:T(8,128)S(1)} %slice_subtract_fusion.3), channel_id=2, replica_groups=mesh['leaf'=8,'row'=4] {'leaf'}, dimensions={2}, use_global_device_ids=true | all-gather | bytes 294912 | tf_op jit(solution)/shard_map/all_gather | solution.py:39
  149.9 1.7 fusion.26
  151.6 30.8 %all_gather.32 = f32[64,1024]{1,0:T(8,128)S(1)} all-gather(f32[64,128]{1,0:T(8,128)S(1)} %fusion.26), channel_id=1, replica_groups=mesh['leaf'=8,'row'=4] {'leaf'}, dimensions={1}, use_global_device_ids=true | all-gather | bytes 294912 | tf_op jit(solution)/shard_map/all_gather | solution.py:43
  182.4 1.7 convolution_subtract_fusion.2
  184.1 31.0 %all_gather.33 = f32[64,1024]{1,0:T(8,128)S(1)} all-gather(f32[64,128]{1,0:T(8,128)S(1)} %convolution_subtract_fusion.2), channel_id=1, replica_groups=mesh['leaf'=8,'row'=4] {'leaf'}, dimensions={1}, use_global_device_ids=true | all-gather | bytes 294912 | tf_op jit(solution)/shard_map/all_gather | solution.py:39
  215.1 0.7 fusion.19
  215.8 30.8 %all_gather.34 = f32[64,1024]{1,0:T(8,128)S(1)} all-gather(f32[64,128]{1,0:T(8,128)S(1)} %fusion.19), channel_id=1, replica_groups=mesh['leaf'=8,'row'=4] {'leaf'}, dimensions={1}, use_global_device_ids=true | all-gather | bytes 294912 | tf_op jit(solution)/shard_map/all_gather | solution.py:43
  246.5 1.4 convolution_subtract_fusion.1
  248.0 30.7 %all_gather.35 = f32[64,1024]{1,0:T(8,128)S(1)} all-gather(f32[64,128]{1,0:T(8,128)S(1)} %convolution_subtract_fusion.1), channel_id=1, replica_groups=mesh['leaf'=8,'row'=4] {'leaf'}, dimensions={1}, use_global_device_ids=true | all-gather | bytes 294912 | tf_op jit(solution)/shard_map/all_gather | solution.py:39
  278.7 0.7 fusion.12
  279.4 30.7 %all_gather.36 = f32[64,1024]{1,0:T(8,128)S(1)} all-gather(f32[64,128]{1,0:T(8,128)S(1)} %fusion.12), channel_id=1, replica_groups=mesh['leaf'=8,'row'=4] {'leaf'}, dimensions={1}, use_global_device_ids=true | all-gather | bytes 294912 | tf_op jit(solution)/shard_map/all_gather | solution.py:43
  310.1 1.4 convolution_subtract_fusion
  311.5 30.7 %all_gather.37 = f32[64,1024]{1,0:T(8,128)S(1)} all-gather(f32[64,128]{1,0:T(8,128)S(1)} %convolution_subtract_fusion), channel_id=1, replica_groups=mesh['leaf'=8,'row'=4] {'leaf'}, dimensions={1}, use_global_device_ids=true | all-gather | bytes 294912 | tf_op jit(solution)/shard_map/all_gather | solution.py:39
  342.3 0.7 fusion.5
  342.9 1.0 fusion.3
  343.9 0.0 reduce-scatter.10.cloned.1.call-update
  344.0 0.0 reduce-scatter.12.cloned.1.call-start
  344.0 53.8 %reduce-scatter.10.cloned.1.call-done = f32[16,128]{1,0:T(8,128)} async-done(((f32[16,1024]{1,0:T(8,128)}), f32[16,128]{1,0:T(8,128)}) %reduce-scatter.10.cloned.1.call-update) | async-done | bytes 8208 | tf_op jit(solution)/shard_map/reduce_scatter | solution.py:55
  397.8 2.1 fusion.7
  399.9 0.0 reduce-scatter.12.cloned.1.call-update
  399.9 0.0 reduce-scatter.14.cloned.1.call-start
  399.9 54.2 %reduce-scatter.12.cloned.1.call-done = f32[16,128]{1,0:T(8,128)} async-done(((f32[16,1024]{1,0:T(8,128)}), f32[16,128]{1,0:T(8,128)}) %reduce-scatter.12.cloned.1.call-update) | async-done | bytes 8208 | tf_op jit(solution)/shard_map/reduce_scatter | solution.py:51
  454.1 2.1 fusion.10
  456.2 0.0 reduce-scatter.14.cloned.1.call-update
  456.2 0.0 reduce-scatter.16.cloned.1.call-start
  456.2 54.2 %reduce-scatter.14.cloned.1.call-done = f32[16,128]{1,0:T(8,128)} async-done(((f32[16,1024]{1,0:T(8,128)}), f32[16,128]{1,0:T(8,128)}) %reduce-scatter.14.cloned.1.call-update) | async-done | bytes 8208 | tf_op jit(solution)/shard_map/reduce_scatter | solution.py:55
  510.4 2.1 fusion.14
  512.5 0.0 reduce-scatter.16.cloned.1.call-update
  512.5 0.0 reduce-scatter.18.cloned.1.call-start
  512.6 54.2 %reduce-scatter.16.cloned.1.call-done = f32[16,128]{1,0:T(8,128)} async-done(((f32[16,1024]{1,0:T(8,128)}), f32[16,128]{1,0:T(8,128)}) %reduce-scatter.16.cloned.1.call-update) | async-done | bytes 8208 | tf_op jit(solution)/shard_map/reduce_scatter | solution.py:51
  566.7 2.1 fusion.17
  568.8 0.0 reduce-scatter.18.cloned.1.call-update
  568.8 0.0 reduce-scatter.20.cloned.1.call-start
  568.9 54.3 %reduce-scatter.18.cloned.1.call-done = f32[16,128]{1,0:T(8,128)} async-done(((f32[16,1024]{1,0:T(8,128)}), f32[16,128]{1,0:T(8,128)}) %reduce-scatter.18.cloned.1.call-update) | async-done | bytes 8208 | tf_op jit(solution)/shard_map/reduce_scatter | solution.py:55
  623.2 2.1 fusion.21
  625.3 0.0 reduce-scatter.20.cloned.1.call-update
  625.3 0.0 reduce-scatter.22.cloned.1.call-start
  625.3 54.3 %reduce-scatter.20.cloned.1.call-done = f32[16,128]{1,0:T(8,128)} async-done(((f32[16,1024]{1,0:T(8,128)}), f32[16,128]{1,0:T(8,128)}) %reduce-scatter.20.cloned.1.call-update) | async-done | bytes 8208 | tf_op jit(solution)/shard_map/reduce_scatter | solution.py:51
  679.7 2.1 fusion.24
  681.7 0.0 reduce-scatter.22.cloned.1.call-update
  681.7 0.0 all-gather.3.cloned.1.call-start
  681.8 54.4 %reduce-scatter.22.cloned.1.call-done = f32[16,128]{1,0:T(8,128)} async-done(((f32[16,1024]{1,0:T(8,128)}), f32[16,128]{1,0:T(8,128)}) %reduce-scatter.22.cloned.1.call-update) | async-done | bytes 8208 | tf_op jit(solution)/shard_map/reduce_scatter | solution.py:55
  736.2 0.7 pad_maximum_fusion
  736.9 5.9 all_gather.38
  742.8 0.0 all-gather.3.cloned.1.call-update
  742.8 0.0 reduce-scatter.24.cloned.1.call-start
  742.9 38.7 %all-gather.3.cloned.1.call-done = f32[4,64,1024]{2,1,0:T(8,128)} async-done(((f32[4,64,128]{2,1,0:T(8,128)}), f32[4,64,1024]{2,1,0:T(8,128)}) %all-gather.3.cloned.1.call-update) | async-done | bytes 1048592 | tf_op jit(solution)/shard_map/all_gather | solution.py:57
  781.6 2.7 fusion.1
  784.3 0.9 fusion.60
  785.2 0.0 reduce-scatter.24.cloned.1.call-update
  785.2 18.6 %reduce-scatter.24.cloned.1.call-done = f32[64,128]{1,0:T(8,128)} async-done(((f32[64,512]{1,0:T(8,128)}), f32[64,128]{1,0:T(8,128)}) %reduce-scatter.24.cloned.1.call-update) | async-done | bytes 32784 | tf_op jit(solution)/shard_map/reduce_scatter | solution.py:61
  803.9 0.7 copy.11
  (16 shorter events, 0.0 us)
Async XLA Ops:
  7.2 8.9 %copy-start = (f32[4,1024,128]{2,1,0:T(8,128)S(1)}, f32[4,1024,128]{2,1,0:T(8,128)}, u32[]{:S(2)}) copy-start(f32[4,1024,128]{2,1,0:T(8,128)} %param.12) | copy-start | bytes 6291460
  7.2 77.9 %reduce-scatter.26.cloned.1.call-start = ((), (), s32[]{:S(2)}) async-start(), calls=%async_computation.18 | async-start | bytes 1179648 | tf_op jit(solution)/shard_map/reduce_scatter | solution.py:32
  16.1 101.9 %copy-start.5 = (f32[4,64,128]{2,1,0:T(8,128)S(1)}, f32[4,64,128]{2,1,0:T(8,128)}, u32[]{:S(2)}) copy-start(f32[4,64,128]{2,1,0:T(8,128)} %param.9) | copy-start | bytes 393220
  19.5 98.5 %all-reduce.2.cloned.1.call-start = ((), (), s32[]{:S(2)}) async-start(), calls=%async_computation.19 | async-start | bytes 262144 | tf_op jit(solution)/shard_map/psum | solution.py:31
  85.1 312.7 %reduce-scatter.10.cloned.1.call-start = ((), (), s32[]{:S(2)}) async-start(), calls=%async_computation.9 | async-start | bytes 73728 | tf_op jit(solution)/shard_map/reduce_scatter | solution.py:55
  118.0 97.2 %copy-start.1 = (f32[4,128,1024]{2,1,0:T(8,128)S(1)}, f32[4,128,1024]{2,1,0:T(8,128)}, u32[]{:S(2)}) copy-start(f32[4,128,1024]{2,1,0:T(8,128)} %param.10) | copy-start | bytes 6291460
  118.0 128.6 %copy-start.2 = (f32[3,128,1024]{2,1,0:T(8,128)S(1)}, f32[3,128,1024]{2,1,0:T(8,128)}, u32[]{:S(2)}) copy-start(f32[3,128,1024]{2,1,0:T(8,128)} %param.11) | copy-start | bytes 4718596
  344.0 110.2 %reduce-scatter.12.cloned.1.call-start = ((), (), s32[]{:S(2)}) async-start(), calls=%async_computation.10 | async-start | bytes 73728 | tf_op jit(solution)/shard_map/reduce_scatter | solution.py:51
  397.8 338.4 %copy-start.6 = (f32[16,128]{1,0:T(8,128)S(1)}, f32[16,128]{1,0:T(8,128)}, u32[]{:S(2)}) copy-start(f32[16,128]{1,0:T(8,128)} %reduce-scatter.10.cloned.1.call-done) | copy-start | bytes 24580
  399.9 110.5 %reduce-scatter.14.cloned.1.call-start = ((), (), s32[]{:S(2)}) async-start(), calls=%async_computation.11 | async-start | bytes 73728 | tf_op jit(solution)/shard_map/reduce_scatter | solution.py:55
  456.2 110.5 %reduce-scatter.16.cloned.1.call-start = ((), (), s32[]{:S(2)}) async-start(), calls=%async_computation.12 | async-start | bytes 73728 | tf_op jit(solution)/shard_map/reduce_scatter | solution.py:51
  510.4 225.8 %copy-start.7 = (f32[16,128]{1,0:T(8,128)S(1)}, f32[16,128]{1,0:T(8,128)}, u32[]{:S(2)}) copy-start(f32[16,128]{1,0:T(8,128)} %reduce-scatter.14.cloned.1.call-done) | copy-start | bytes 24580
  512.5 110.7 %reduce-scatter.18.cloned.1.call-start = ((), (), s32[]{:S(2)}) async-start(), calls=%async_computation.13 | async-start | bytes 73728 | tf_op jit(solution)/shard_map/reduce_scatter | solution.py:55
  568.8 110.8 %reduce-scatter.20.cloned.1.call-start = ((), (), s32[]{:S(2)}) async-start(), calls=%async_computation.14 | async-start | bytes 73728 | tf_op jit(solution)/shard_map/reduce_scatter | solution.py:51
  625.3 159.0 %copy-start.4 = (f32[128,512]{1,0:T(8,128)S(1)}, f32[128,512]{1,0:T(8,128)}, u32[]{:S(2)}) copy-start(f32[128,512]{1,0:T(8,128)} %param.8) | copy-start | bytes 786436
  625.3 110.9 %reduce-scatter.22.cloned.1.call-start = ((), (), s32[]{:S(2)}) async-start(), calls=%async_computation.15 | async-start | bytes 73728 | tf_op jit(solution)/shard_map/reduce_scatter | solution.py:55
  681.7 99.8 %all-gather.3.cloned.1.call-start = ((), (), s32[]{:S(2)}) async-start(), calls=%async_computation.16 | async-start | bytes 1179648 | tf_op jit(solution)/shard_map/all_gather | solution.py:57
  742.8 61.1 %copy-start.3 = (f32[4,64,128]{2,1,0:T(8,128)S(1)}, f32[4,64,128]{2,1,0:T(8,128)}, u32[]{:S(2)}) copy-start(f32[4,64,128]{2,1,0:T(8,128)} %all_gather.38) | copy-start | bytes 393220
  742.8 61.0 %reduce-scatter.24.cloned.1.call-start = ((), (), s32[]{:S(2)}) async-start(), calls=%async_computation.17 | async-start | bytes 163840 | tf_op jit(solution)/shard_map/reduce_scatter | solution.py:61
Sparse Core Ops, SparseCore 0:
  19.6 65.4 reduce-scatter.25
  87.5 30.4 all-reduce.1
  344.1 53.6 reduce-scatter.9
  401.4 52.7 reduce-scatter.11
  457.7 52.7 reduce-scatter.13
  514.0 52.7 reduce-scatter.15
  570.4 52.7 reduce-scatter.17
  626.9 52.7 reduce-scatter.19
  683.4 52.7 reduce-scatter.21
  742.9 38.5 all-gather.2
  785.4 18.4 reduce-scatter.23
where the time goes:
time: 812 us; the launch traced here: 811 us
  waiting for transfers between devices  535 us (66%)
  blocking collectives  229 us (28%)
  matrix products  29.9 us (4%)
  between operations  14 us (2%)
    reduce_scatter x4, waiting for transfers between devices, per_device(): lax.psum_scatter(solve_part, 'leaf', scatter_dimension=1, tiled=True)  217 us
    reduce_scatter x3, waiting for transfers between devices, per_device(): lax.psum_scatter(coupling_part, 'leaf', scatter_dimension=1, tiled=True)  163 us
    all_gather x4, blocking collectives, per_device(): known_full = lax.all_gather(known_part, 'leaf', axis=1, tiled=True)  123 us
    all_gather x3, blocking collectives, per_device(): y_full = lax.all_gather(y_level, 'leaf', axis=1, tiled=True)  92.3 us
    reduce_scatter x1, waiting for transfers between devices, per_device(): lax.psum_scatter(row_total, 'leaf', scatter_dimension=2, tiled=True)  65.5 us
    all_gather x1, waiting for transfers between devices, per_device(): solved_full = lax.all_gather(solved_stack, 'leaf', axis=2, tiled=True)  38.7 us
    psum x1, waiting for transfers between devices, per_device(): row_total = lax.psum(section_parts, 'row')  32.8 us
    reduce_scatter x1, waiting for transfers between devices, per_device(): lax.psum_scatter(section_part, 'row', scatter_dimension=1, tiled=True)  18.6 us
  transfers between devices with their start and end apart: 11, of which 11 were waited for; matrix products, arithmetic and copies ran while one was open for 0% of the time, Pallas kernels for 0%

commit v1 on v0

--- a/solution.py
+++ b/solution.py
@@ -2,6 +2,18 @@
 import jax.numpy as jnp
 from jax import lax
 from jax.sharding import PartitionSpec as P
+
+
+def doubled_up(array, axis, dim):
+    ways, here = (lax.axis_size(axis), lax.axis_index(axis))
+    grown, reach = (array, 1)
+    while reach < ways:
+        theirs = lax.ppermute(grown, axis, [(d, d ^ reach) for d in range(ways)])
+        mine_first = jnp.concatenate([grown, theirs], axis=dim)
+        theirs_first = jnp.concatenate([theirs, grown], axis=dim)
+        grown = jnp.where(here & reach == 0, mine_first, theirs_first)
+        reach = 2 * reach
+    return grown
 
 
 def dot_last(left, right):
@@ -36,7 +48,7 @@
         known_part = sep_rhs[level] - reduced[level]
         if level > 0:
             known_part = known_part - dot_last(y_full, sep_coupling[level - 1])
-        known_full = lax.all_gather(known_part, "leaf", axis=1, tiled=True)
+        known_full = doubled_up(known_part, "leaf", 1)
         y_level = dot_last(known_full, sep_inverse[level])
         y_leaf.append(y_level)
         if level < levels - 1:

time: 812 us -> 753 us (0.927)
  blocking collectives: 229 us -> 105 us
  waiting for transfers between devices: 535 us -> 586 us
  starting transfers between devices: 0.45 us -> 11.3 us
    all_gather x4 -> x0, blocking collectives: 123 us -> none  [per_device(): known_full = lax.all_gather(known_part, 'leaf', axis=1, tiled=True)]
    ppermute x0 -> x12, waiting for transfers between devices: none -> 51.2 us  [doubled_up(): theirs = lax.ppermute(grown, axis, [(d, d ^ reach) for d in range(ways)])]
    ppermute x0 -> x12, starting transfers between devices: none -> 10.9 us  [doubled_up(): theirs = lax.ppermute(grown, axis, [(d, d ^ reach) for d in range(ways)])]
  transfers between devices with their start and end apart: 11 -> 23, of which waited for: 11 -> 23; matrix products, arithmetic and copies ran while one was open for 0% -> 0% of each run, Pallas kernels for 0% -> 0%
where the time goes in v1:
time: 753 us; the launch traced here: 752 us
  waiting for transfers between devices  586 us (78%)
  blocking collectives  105 us (14%)
  matrix products  32.6 us (4%)
  between operations  14 us (2%)
  starting transfers between devices  11.3 us (2%)
    reduce_scatter x4, waiting for transfers between devices, per_device(): lax.psum_scatter(solve_part, 'leaf', scatter_dimension=1, tiled=True)  216 us
    reduce_scatter x3, waiting for transfers between devices, per_device(): lax.psum_scatter(coupling_part, 'leaf', scatter_dimension=1, tiled=True)  163 us
    all_gather x3, blocking collectives, per_device(): y_full = lax.all_gather(y_level, 'leaf', axis=1, tiled=True)  92.7 us
    reduce_scatter x1, waiting for transfers between devices, per_device(): lax.psum_scatter(row_total, 'leaf', scatter_dimension=2, tiled=True)  65.5 us
    ppermute x12, waiting for transfers between devices, doubled_up(): theirs = lax.ppermute(grown, axis, [(d, d ^ reach) for d in range(ways)])  51.2 us
    all_gather x1, waiting for transfers between devices, per_device(): solved_full = lax.all_gather(solved_stack, 'leaf', axis=2, tiled=True)  38.7 us
    psum x1, waiting for transfers between devices, per_device(): row_total = lax.psum(section_parts, 'row')  32.8 us
    reduce_scatter x1, waiting for transfers between devices, per_device(): lax.psum_scatter(section_part, 'row', scatter_dimension=1, tiled=True)  18.6 us
  transfers between devices with their start and end apart: 23, of which 23 were waited for; matrix products, arithmetic and copies ran while one was open for 0% of the time, Pallas kernels for 0%

profile of v1, /device:TPU:0, one launch (start us, length us, event | category | flops | bytes accessed | tf_op | source)
XLA Modules:
  0.0 752.4 jit_solution(203915319454554147)
XLA Ops:
  7.2 6.9 all_gather.18
  14.1 0.7 convert_bitcast_fusion
  14.7 1.3 fusion.87
  16.1 3.4 fusion
  19.5 65.5 %reduce-scatter.26.cloned.1.call-done = f32[4,64,128]{2,1,0:T(8,128)} async-done(((f32[4,64,1024]{2,1,0:T(8,128)}), f32[4,64,128]{2,1,0:T(8,128)}) %reduce-scatter.26.cloned.1.call-update) | async-done | bytes 131088 | tf_op jit(solution)/shard_map/reduce_scatter | solution.py:44
  85.2 32.8 %all-reduce.2.cloned.1.call-done = f32[4,64,128]{2,1,0:T(8,128)} async-done(((f32[4,64,128]{2,1,0:T(8,128)}), f32[4,64,128]{2,1,0:T(8,128)}) %all-reduce.2.cloned.1.call-update) | async-done | bytes 131088 | tf_op jit(solution)/shard_map/psum | solution.py:43
  118.0 0.8 fusion.70
  118.8 1.5 collective-permute-start
  120.3 2.4 collective-permute-done
  122.7 1.6 collective-permute-start.1
  124.3 4.0 collective-permute-done.1
  128.3 2.0 collective-permute-start.2
  130.3 5.1 collective-permute-done.2
  135.4 1.7 fusion.26
  137.1 30.7 %all_gather.19 = f32[64,1024]{1,0:T(8,128)S(1)} all-gather(f32[64,128]{1,0:T(8,128)S(1)} %fusion.26), channel_id=1, replica_groups=mesh['leaf'=8,'row'=4] {'leaf'}, dimensions={1}, use_global_device_ids=true | all-gather | bytes 294912 | tf_op jit(solution)/shard_map/all_gather | solution.py:55
  167.8 1.7 convolution_subtract_fusion.2
  169.5 0.9 collective-permute-start.3
  170.4 3.1 collective-permute-done.3
  173.5 0.1 collective-permute-start.4
  173.6 4.3 collective-permute-done.4
  177.9 0.7 collective-permute-start.5
  178.6 6.2 collective-permute-done.5
  184.8 0.7 fusion.19
  185.5 31.0 %all_gather.20 = f32[64,1024]{1,0:T(8,128)S(1)} all-gather(f32[64,128]{1,0:T(8,128)S(1)} %fusion.19), channel_id=1, replica_groups=mesh['leaf'=8,'row'=4] {'leaf'}, dimensions={1}, use_global_device_ids=true | all-gather | bytes 294912 | tf_op jit(solution)/shard_map/all_gather | solution.py:55
  216.6 1.7 convolution_subtract_fusion.1
  218.3 1.2 collective-permute-start.6
  219.4 2.8 collective-permute-done.6
  222.3 0.1 collective-permute-start.7
  222.3 4.3 collective-permute-done.7
  226.6 0.9 collective-permute-start.8
  227.6 6.0 collective-permute-done.8
  233.6 0.7 fusion.12
  234.2 31.0 %all_gather.21 = f32[64,1024]{1,0:T(8,128)S(1)} all-gather(f32[64,128]{1,0:T(8,128)S(1)} %fusion.12), channel_id=1, replica_groups=mesh['leaf'=8,'row'=4] {'leaf'}, dimensions={1}, use_global_device_ids=true | all-gather | bytes 294912 | tf_op jit(solution)/shard_map/all_gather | solution.py:55
  265.2 1.7 convolution_subtract_fusion
  266.9 1.1 collective-permute-start.9
  268.0 2.9 collective-permute-done.9
  270.9 0.1 collective-permute-start.10
  271.0 4.3 collective-permute-done.10
  275.2 0.9 collective-permute-start.11
  276.1 5.9 collective-permute-done.11
  282.0 1.7 fusion.5
  283.7 2.0 fusion.3
  285.8 0.0 reduce-scatter.12.cloned.1.call-start
  285.9 53.3 %reduce-scatter.10.cloned.1.call-done = f32[16,128]{1,0:T(8,128)} async-done(((f32[16,1024]{1,0:T(8,128)}), f32[16,128]{1,0:T(8,128)}) %reduce-scatter.10.cloned.1.call-update) | async-done | bytes 8208 | tf_op jit(solution)/shard_map/reduce_scatter | solution.py:67
  339.2 2.1 fusion.7
  341.3 54.2 %reduce-scatter.12.cloned.1.call-done = f32[16,128]{1,0:T(8,128)} async-done(((f32[16,1024]{1,0:T(8,128)}), f32[16,128]{1,0:T(8,128)}) %reduce-scatter.12.cloned.1.call-update) | async-done | bytes 8208 | tf_op jit(solution)/shard_map/reduce_scatter | solution.py:63
  395.5 2.1 fusion.10
  397.6 54.2 %reduce-scatter.14.cloned.1.call-done = f32[16,128]{1,0:T(8,128)} async-done(((f32[16,1024]{1,0:T(8,128)}), f32[16,128]{1,0:T(8,128)}) %reduce-scatter.14.cloned.1.call-update) | async-done | bytes 8208 | tf_op jit(solution)/shard_map/reduce_scatter | solution.py:67
  451.8 2.1 fusion.14
  453.9 54.2 %reduce-scatter.16.cloned.1.call-done = f32[16,128]{1,0:T(8,128)} async-done(((f32[16,1024]{1,0:T(8,128)}), f32[16,128]{1,0:T(8,128)}) %reduce-scatter.16.cloned.1.call-update) | async-done | bytes 8208 | tf_op jit(solution)/shard_map/reduce_scatter | solution.py:63
  508.1 2.1 fusion.17
  510.2 0.0 reduce-scatter.20.cloned.1.call-start
  510.2 54.3 %reduce-scatter.18.cloned.1.call-done = f32[16,128]{1,0:T(8,128)} async-done(((f32[16,1024]{1,0:T(8,128)}), f32[16,128]{1,0:T(8,128)}) %reduce-scatter.18.cloned.1.call-update) | async-done | bytes 8208 | tf_op jit(solution)/shard_map/reduce_scatter | solution.py:67
  564.6 2.1 fusion.21
  566.7 54.3 %reduce-scatter.20.cloned.1.call-done = f32[16,128]{1,0:T(8,128)} async-done(((f32[16,1024]{1,0:T(8,128)}), f32[16,128]{1,0:T(8,128)}) %reduce-scatter.20.cloned.1.call-update) | async-done | bytes 8208 | tf_op jit(solution)/shard_map/reduce_scatter | solution.py:63
  621.0 2.1 fusion.24
  623.1 54.4 %reduce-scatter.22.cloned.1.call-done = f32[16,128]{1,0:T(8,128)} async-done(((f32[16,1024]{1,0:T(8,128)}), f32[16,128]{1,0:T(8,128)}) %reduce-scatter.22.cloned.1.call-update) | async-done | bytes 8208 | tf_op jit(solution)/shard_map/reduce_scatter | solution.py:67
  677.5 0.7 pad_maximum_fusion
  678.2 5.9 all_gather.22
  684.2 38.7 %all-gather.2.cloned.1.call-done = f32[4,64,1024]{2,1,0:T(8,128)} async-done(((f32[4,64,128]{2,1,0:T(8,128)}), f32[4,64,1024]{2,1,0:T(8,128)}) %all-gather.2.cloned.1.call-update) | async-done | bytes 1048592 | tf_op jit(solution)/shard_map/all_gather | solution.py:69
  722.9 2.7 fusion.1
  725.6 0.9 fusion.88
  726.6 18.6 %reduce-scatter.24.cloned.1.call-done = f32[64,128]{1,0:T(8,128)} async-done(((f32[64,512]{1,0:T(8,128)}), f32[64,128]{1,0:T(8,128)}) %reduce-scatter.24.cloned.1.call-update) | async-done | bytes 32784 | tf_op jit(solution)/shard_map/reduce_scatter | solution.py:73
  745.2 0.7 copy.11
  (44 shorter events, 0.7 us)
Async XLA Ops:
  7.2 8.9 %copy-start = (f32[4,1024,128]{2,1,0:T(8,128)S(1)}, f32[4,1024,128]{2,1,0:T(8,128)}, u32[]{:S(2)}) copy-start(f32[4,1024,128]{2,1,0:T(8,128)} %param.12) | copy-start | bytes 6291460
  7.2 77.9 %reduce-scatter.26.cloned.1.call-start = ((), (), s32[]{:S(2)}) async-start(), calls=%async_computation.18 | async-start | bytes 1179648 | tf_op jit(solution)/shard_map/reduce_scatter | solution.py:44
  16.1 101.9 %copy-start.4 = (f32[4,64,128]{2,1,0:T(8,128)S(1)}, f32[4,64,128]{2,1,0:T(8,128)}, u32[]{:S(2)}) copy-start(f32[4,64,128]{2,1,0:T(8,128)} %param.9) | copy-start | bytes 393220
  19.5 98.5 %all-reduce.2.cloned.1.call-start = ((), (), s32[]{:S(2)}) async-start(), calls=%async_computation.19 | async-start | bytes 262144 | tf_op jit(solution)/shard_map/psum | solution.py:43
  85.1 254.0 %reduce-scatter.10.cloned.1.call-start = ((), (), s32[]{:S(2)}) async-start(), calls=%async_computation.9 | async-start | bytes 73728 | tf_op jit(solution)/shard_map/reduce_scatter | solution.py:67
  118.0 98.6 %copy-start.5 = (f32[4,64,128]{2,1,0:T(8,128)S(1)}, f32[4,64,128]{2,1,0:T(8,128)}, u32[]{:S(2)}) copy-start(f32[4,64,128]{2,1,0:T(8,128)} %all-reduce.2.cloned.1.call-done) | copy-start | bytes 393220
  118.8 3.9 collective-permute-start
  122.7 5.5 collective-permute-start.1
  128.3 7.1 collective-permute-start.2
  130.3 54.6 %copy-start.1 = (f32[4,128,1024]{2,1,0:T(8,128)S(1)}, f32[4,128,1024]{2,1,0:T(8,128)}, u32[]{:S(2)}) copy-start(f32[4,128,1024]{2,1,0:T(8,128)} %param.10) | copy-start | bytes 6291460
  169.5 4.0 collective-permute-start.3
  173.5 4.3 collective-permute-start.4
  177.9 7.0 collective-permute-start.5
  218.3 4.0 collective-permute-start.6
  222.3 4.3 collective-permute-start.7
  226.6 7.0 collective-permute-start.8
  266.9 4.0 collective-permute-start.9
  270.9 4.3 collective-permute-start.10
  275.2 6.8 collective-permute-start.11
  285.8 109.7 %reduce-scatter.12.cloned.1.call-start = ((), (), s32[]{:S(2)}) async-start(), calls=%async_computation.10 | async-start | bytes 73728 | tf_op jit(solution)/shard_map/reduce_scatter | solution.py:63
  339.2 338.4 %copy-start.6 = (f32[16,128]{1,0:T(8,128)S(1)}, f32[16,128]{1,0:T(8,128)}, u32[]{:S(2)}) copy-start(f32[16,128]{1,0:T(8,128)} %reduce-scatter.10.cloned.1.call-done) | copy-start | bytes 24580
  341.3 110.5 %reduce-scatter.14.cloned.1.call-start = ((), (), s32[]{:S(2)}) async-start(), calls=%async_computation.11 | async-start | bytes 73728 | tf_op jit(solution)/shard_map/reduce_scatter | solution.py:67
  397.6 110.5 %reduce-scatter.16.cloned.1.call-start = ((), (), s32[]{:S(2)}) async-start(), calls=%async_computation.12 | async-start | bytes 73728 | tf_op jit(solution)/shard_map/reduce_scatter | solution.py:63
  451.8 225.7 %copy-start.7 = (f32[16,128]{1,0:T(8,128)S(1)}, f32[16,128]{1,0:T(8,128)}, u32[]{:S(2)}) copy-start(f32[16,128]{1,0:T(8,128)} %reduce-scatter.14.cloned.1.call-done) | copy-start | bytes 24580
  453.9 110.7 %reduce-scatter.18.cloned.1.call-start = ((), (), s32[]{:S(2)}) async-start(), calls=%async_computation.13 | async-start | bytes 73728 | tf_op jit(solution)/shard_map/reduce_scatter | solution.py:67
  510.2 110.8 %reduce-scatter.20.cloned.1.call-start = ((), (), s32[]{:S(2)}) async-start(), calls=%async_computation.14 | async-start | bytes 73728 | tf_op jit(solution)/shard_map/reduce_scatter | solution.py:63
  566.6 159.0 %copy-start.3 = (f32[128,512]{1,0:T(8,128)S(1)}, f32[128,512]{1,0:T(8,128)}, u32[]{:S(2)}) copy-start(f32[128,512]{1,0:T(8,128)} %param.8) | copy-start | bytes 786436
  566.6 110.9 %reduce-scatter.22.cloned.1.call-start = ((), (), s32[]{:S(2)}) async-start(), calls=%async_computation.15 | async-start | bytes 73728 | tf_op jit(solution)/shard_map/reduce_scatter | solution.py:67
  623.1 99.8 %all-gather.2.cloned.1.call-start = ((), (), s32[]{:S(2)}) async-start(), calls=%async_computation.16 | async-start | bytes 1179648 | tf_op jit(solution)/shard_map/all_gather | solution.py:69
  684.1 61.1 %copy-start.2 = (f32[4,64,128]{2,1,0:T(8,128)S(1)}, f32[4,64,128]{2,1,0:T(8,128)}, u32[]{:S(2)}) copy-start(f32[4,64,128]{2,1,0:T(8,128)} %all_gather.22) | copy-start | bytes 393220
  684.2 61.0 %reduce-scatter.24.cloned.1.call-start = ((), (), s32[]{:S(2)}) async-start(), calls=%async_computation.17 | async-start | bytes 163840 | tf_op jit(solution)/shard_map/reduce_scatter | solution.py:73
Sparse Core Ops, SparseCore 0:
  19.6 65.4 reduce-scatter.25
  87.5 30.4 all-reduce.1
  285.9 53.1 reduce-scatter.9
  342.7 52.7 reduce-scatter.11
  399.0 52.7 reduce-scatter.13
  455.3 52.7 reduce-scatter.15
  511.8 52.7 reduce-scatter.17
  568.3 52.7 reduce-scatter.19
  624.7 52.7 reduce-scatter.21
  684.3 38.5 all-gather.1
  726.7 18.4 reduce-scatter.23
